TPU v7x, 32 devices: a whole 2x2x4 slice. The times are simulated.
32 devices in a mesh: groups: 2 (over y), tensor: 4 (over x, core), pool: 4 (over z).
Axes of the slice: x: 2, y: 2, z: 4, core: 2. Of those that a mesh axis runs over, the one named last changes fastest.
Arguments:
- queries: bfloat16 [1024, 8192], P(('groups', 'tensor'), 'pool'), parts along dimension 0
- key_value_cache: bfloat16 [1024, 128, 2, 1024], P(('groups', 'tensor'), None, None, 'pool'), parts along dimension 0
- cache_lengths: int32 [1024], P(('groups', 'tensor')), parts along dimension 0, may hold values from 1 to 128
- block_adapter_slot: int32 [8], P('groups'), parts along dimension 0, may hold values from 0 to 7, as said below
- output_weight: bfloat16 [8192, 8192], P('pool', 'tensor'), may hold values from -0.0625 to 0.0625
- adapter_down_weight: bfloat16 [16, 8192, 64], P(('groups', 'tensor'), 'pool'), parts along dimension 0, may hold values from -0.0625 to 0.0625
- adapter_up_weight: bfloat16 [16, 64, 8192], P('groups', 'pool', 'tensor'), parts along dimension 0, may hold values from -0.75 to 0.75
Outputs:
- projected: bfloat16 [1024, 8192], P(('groups', 'pool'), 'tensor'), parts along dimension 0
There are 2 independent parts, one for each index of `groups`. A program takes and returns all parts, laid end to end along the dimension named above; an argument that names none is the same for every part. Nothing has to cross between parts.
Inputs may be any that keep to these rules, and one draw needn't show every extreme that they name: `block_adapter_slot`: block b covers rows b * 128 to (b + 1) * 128 - 1. Each run of 2 slots that starts at a multiple of 2 is named by at least one block.
All inputs are finite; a program needn't handle non-finite values.
Results may differ from a plain program's by a relative error of at most 0.0058.
Values may be sent and summed in bfloat16 or wider, within the bound.
A program may use at most 128 MiB of HBM per device.

v0:
```python
import math

import jax
import jax.numpy as jnp
from jax import lax
from jax.sharding import PartitionSpec as P

H = 64
KVH = 8
HD = 128
BLK = 128


adapter_scale = 2.0


def local_attention(queries, key_value_cache, cache_lengths):
    row_count, feat_width = queries.shape
    positions = key_value_cache.shape[1]
    group_size = H // KVH
    local_kv = key_value_cache.shape[3] // HD
    key_all = key_value_cache[:, :, 0]
    value_all = key_value_cache[:, :, 1]
    visible = (jnp.arange(positions, dtype=jnp.int32)[None, :] < cache_lengths[:, None])[:, None, :]
    outputs = []
    for head in range(local_kv):
        q_rows = queries[:, head * group_size * HD : (head + 1) * group_size * HD].reshape(
            row_count, group_size, HD
        )
        key_rows = key_all[:, :, head * HD : (head + 1) * HD]
        value_rows = value_all[:, :, head * HD : (head + 1) * HD]
        scores = jnp.einsum(
            "rgd,rjd->rgj", q_rows, key_rows, preferred_element_type=jnp.float32
        ) * (1.0 / math.sqrt(HD))
        row_max = jnp.max(jnp.where(visible, scores, -1e30), axis=-1)
        expo_terms = jnp.where(visible, jnp.exp(scores - row_max[..., None]), 0.0)
        totals = jnp.sum(expo_terms, axis=-1)
        weights = expo_terms.astype(jnp.bfloat16)
        mixed_rows = (
            jnp.einsum("rgj,rjd->rgd", weights, value_rows, preferred_element_type=jnp.float32)
            / totals[..., None]
        )
        outputs.append(mixed_rows.reshape(row_count, group_size * HD))
    return jnp.concatenate(outputs, axis=1).astype(jnp.bfloat16)


def local(
    queries,
    key_value_cache,
    cache_lengths,
    block_adapter_slot,
    output_weight,
    adapter_down_weight,
    adapter_up_weight,
):
    attended = local_attention(queries, key_value_cache, cache_lengths)
    row_count, feat_width = attended.shape
    tensor_index = lax.axis_index("tensor")
    per_device = row_count // BLK
    local_slots = lax.dynamic_slice_in_dim(
        block_adapter_slot, tensor_index * per_device, per_device
    )
    slot_range = lax.all_gather(adapter_down_weight, "tensor", axis=0, tiled=True)
    chosen = jnp.take(slot_range, local_slots, axis=0)
    partial_value = jnp.einsum(
        "bnd,bdr->bnr",
        attended.reshape(per_device, BLK, feat_width),
        chosen,
        preferred_element_type=jnp.float32,
    )
    partial_value = partial_value.reshape(row_count, -1)
    rank_share = lax.psum_scatter(partial_value, "pool", scatter_dimension=1, tiled=True).astype(
        jnp.bfloat16
    )
    rank_share_width = adapter_up_weight.shape[1]
    output_columns = adapter_up_weight.shape[2]
    att_piece = lax.all_gather(attended, "tensor", axis=0, tiled=True)
    share_piece = lax.all_gather(rank_share, "tensor", axis=0, tiled=True)
    piece_rows = att_piece.shape[0]
    block_count = piece_rows // BLK
    block_ids = jnp.arange(block_count, dtype=jnp.int32)
    piece_slots = jnp.take(block_adapter_slot, block_ids)
    picked_up = jnp.take(adapter_up_weight, piece_slots, axis=0)
    base_output = jnp.dot(att_piece, output_weight, preferred_element_type=jnp.float32)
    expand_rows = jnp.einsum(
        "bnr,brd->bnd",
        share_piece.reshape(block_count, BLK, rank_share_width),
        picked_up,
        preferred_element_type=jnp.float32,
    )
    expand_rows = expand_rows.reshape(piece_rows, output_columns)
    gathered_rows = base_output + adapter_scale * expand_rows
    return lax.psum_scatter(gathered_rows, "pool", scatter_dimension=0, tiled=True).astype(
        jnp.bfloat16
    )


def solution(mesh):
    in_specs = (
        P(("groups", "tensor"), "pool"),
        P(("groups", "tensor"), None, None, "pool"),
        P(("groups", "tensor")),
        P("groups"),
        P("pool", "tensor"),
        P(("groups", "tensor"), "pool", None),
        P("groups", "pool", "tensor"),
    )
    out_specs = P(("groups", "pool"), "tensor")
    return jax.shard_map(local, mesh=mesh, in_specs=in_specs, out_specs=out_specs, check_vma=False)
```

profile of v0, /device:TPU:0, one launch (start us, length us, event | category | flops | bytes accessed | tf_op | source)
XLA Modules:
  0.0 218.4 jit_solution(11496466099560606035)
XLA Ops:
  6.5 0.7 all-gather.5.cloned.1.call-update
  7.3 32.6 %fusion.51 = (bf16[128,128,1,256]{3,2,1,0:T(2,128)(2,1)S(1)}, bf16[128,128,1,256]{3,2,1,0:T(2,128)(2,1)}) fusion(bf16[128,128,2,256]{3,2,1,0:T(2,128)(2,1)} %param.8), kind=kLoop, calls=%fused_computation.68 | loop fusion | bytes 33554432 | tf_op jit(solution)/shard_map/slice | solution.py:22
  39.9 15.5 %copy_bitcast_fusion = (bf16[128,128,256]{2,1,0:T(8,128)(2,1)}, bf16[128,128,256]{2,1,0:T(8,128)(2,1)}) fusion(bf16[128,128,1,256]{3,2,1,0:T(2,128)(2,1)} %get-tuple-element.17, bf16[128,128,1,256]{3,2,1,0:T(2,128)(2,1)S(1)} %get-tuple-element.16), kind=kLoop, calls=%fused_computation.6 | loop fusion | bytes 33554432 | tf_op jit(solution)/shard_map/squeeze | solution.py:23
  55.4 0.6 dynamic_slice.3
  58.1 0.1 iota_compare_fusion
  58.2 4.4 %fusion.12 = f32[128,8,128]{2,1,0:T(8,128)S(1)} fusion(bf16[128,8,128]{2,1,0:T(8,128)(2,1)S(1)} %bitcast.42, bf16[128,128,256]{2,1,0:T(8,128)(2,1)} %get-tuple-element.21), kind=kOutput, calls=%fused_computation.18 | convolution fusion | flops 33685504 | bytes 4980736 | tf_op jit(solution)/shard_map/rgd,rjd->rgj/dot_general | solution.py:32
  62.6 3.5 %fusion.8 = f32[128,8,128]{2,1,0:T(8,128)S(1)} fusion(bf16[128,128,256]{2,1,0:T(8,128)(2,1)} %get-tuple-element.20, f32[128,8,128]{2,1,0:T(8,128)S(1)} %fusion.12, pred[128,128]{1,0:T(8,128)(4,1)S(1)} %iota_compare_fusion), kind=kOutput, calls=%fused_computation.12 | convolution fusion | flops 34079872 | bytes 5799936 | tf_op jit(solution)/shard_map/rgj,rjd->rgd/dot_general | solution.py:40
  66.1 0.4 fusion.27
  66.6 4.4 %fusion.15 = f32[128,8,128]{2,1,0:T(8,128)S(1)} fusion(bf16[128,8,128]{2,1,0:T(8,128)(2,1)S(1)} %bitcast.41, bf16[128,128,256]{2,1,0:T(8,128)(2,1)} %get-tuple-element.21), kind=kOutput, calls=%fused_computation.19 | convolution fusion | flops 33685504 | bytes 4980736 | tf_op jit(solution)/shard_map/rgd,rjd->rgj/dot_general | solution.py:32
  71.0 3.5 %fusion.4 = f32[128,8,128]{2,1,0:T(8,128)S(1)} fusion(bf16[128,128,256]{2,1,0:T(8,128)(2,1)} %get-tuple-element.20, f32[128,8,128]{2,1,0:T(8,128)S(1)} %fusion.15, pred[128,128]{1,0:T(8,128)(4,1)S(1)} %iota_compare_fusion), kind=kOutput, calls=%fused_computation.8 | convolution fusion | flops 34079872 | bytes 5799936 | tf_op jit(solution)/shard_map/rgj,rjd->rgd/dot_general | solution.py:40
  74.5 0.4 fusion.26
  75.0 2.0 fusion.30
  77.1 0.0 all-gather.3.cloned.1.call-start
  77.1 0.7 all-gather.3.cloned.1.call-update
  77.9 0.6 gather_fusion
  78.5 0.6 gather_fusion.1
  79.1 19.7 %reduce-scatter.3.cloned.1.call-done = f32[128,16]{0,1:T(8,128)} async-done(((f32[128,64]{0,1:T(8,128)}), f32[128,16]{0,1:T(8,128)}) %reduce-scatter.3.cloned.1.call-update) | async-done | bytes 8208 | tf_op jit(solution)/shard_map/reduce_scatter | solution.py:72
  98.8 0.7 convert_element_type.17
  99.5 5.3 %all_gather.11 = bf16[512,16]{0,1:T(8,128)(2,1)S(1)} all-gather(bf16[128,16]{0,1:T(8,128)(2,1)S(1)} %convert_element_type.17), channel_id=1, replica_groups=mesh['groups'=2,'tensor'=4,'pool'=4] {'tensor'}, dimensions={0}, use_global_device_ids=true | all-gather | bytes 20480 | tf_op jit(solution)/shard_map/all_gather | solution.py:78
  104.8 2.7 %convolution_multiply_fusion = f32[4,128,2048]{2,1,0:T(8,128)} fusion(bf16[4,16,2048]{2,1,0:T(8,128)(2,1)S(1)} %gather_fusion.1, pred[4]{0:T(512)(128)(4,1)S(1)} %compare_and_fusion, bf16[512,16]{0,1:T(8,128)(2,1)S(1)} %all_gather.11), kind=kOutput, calls=%fused_computation.17 | convolution fusion | flops 34734080 | bytes 4472836 | tf_op jit(solution)/shard_map/bnr,brd->bnd/dot_general | solution.py:85
  107.6 13.7 %all-gather.3.cloned.1.call-done = bf16[512,2048]{1,0:T(8,128)(2,1)} async-done(((bf16[128,2048]{1,0:T(8,128)(2,1)}), bf16[512,2048]{1,0:T(8,128)(2,1)}) %all-gather.3.cloned.1.call-update) | async-done | bytes 2097168 | tf_op jit(solution)/shard_map/all_gather | solution.py:77
  121.3 11.6 %bitcast_add_fusion = f32[512,2048]{1,0:T(8,128)} fusion(f32[4,128,2048]{2,1,0:T(8,128)} %convolution_multiply_fusion, bf16[512,2048]{1,0:T(8,128)(2,1)} %all-gather.3.cloned.1.call-done, bf16[2048,2048]{1,0:T(8,128)(2,1)} %param.11), kind=kOutput, calls=%fused_computation.16 | convolution fusion | flops 4296015872 | bytes 18874368 | tf_op jit(solution)/shard_map/dot_general | solution.py:84
  132.9 76.9 %reduce-scatter.5.cloned.1.call-done = f32[128,2048]{1,0:T(8,128)} async-done(((f32[512,2048]{1,0:T(8,128)}), f32[128,2048]{1,0:T(8,128)}) %reduce-scatter.5.cloned.1.call-update) | async-done | bytes 1048592 | tf_op jit(solution)/shard_map/reduce_scatter | solution.py:93
  209.8 2.1 convert_element_type.18
  (26 shorter events, 0.4 us)
Async XLA Ops:
  6.5 72.0 %copy-start = (bf16[8,16,2048]{2,1,0:T(8,128)(2,1)S(1)}, bf16[8,16,2048]{2,1,0:T(8,128)(2,1)}, u32[]{:S(2)}) copy-start(bf16[8,16,2048]{2,1,0:T(8,128)(2,1)} %param.13) | copy-start | bytes 1572868
  6.5 68.5 %all-gather.5.cloned.1.call-start = ((), (), s32[]{:S(2)}) async-start(), calls=%async_computation.3 | async-start | bytes 2621440 | tf_op jit(solution)/shard_map/all_gather | solution.py:63
  7.3 91.5 %reduce-scatter.3.cloned.1.call-start = ((), (), s32[]{:S(2)}) async-start(), calls=%async_computation.4 | async-start | bytes 40960 | tf_op jit(solution)/shard_map/reduce_scatter | solution.py:72
  39.9 15.5 %copy-start.1 = (s32[4]{0:T(128)S(1)}, s32[4]{0:T(128)}, u32[]{:S(2)}) copy-start(s32[4]{0:T(128)} %param.10) | copy-start | bytes 52
  39.9 18.1 %copy-start.3 = (bf16[128,2048]{1,0:T(8,128)(2,1)S(1)}, bf16[128,2048]{1,0:T(8,128)(2,1)}, u32[]{:S(2)}) copy-start(bf16[128,2048]{1,0:T(8,128)(2,1)} %param.7) | copy-start | bytes 1572868
  39.9 18.2 %copy-start.4 = (s32[128]{0:T(128)S(1)}, s32[128]{0:T(128)}, u32[]{:S(2)}) copy-start(s32[128]{0:T(128)} %param.9) | copy-start | bytes 1540
  75.0 2.1 copy-start.2
  77.1 44.2 %all-gather.3.cloned.1.call-start = ((), (), s32[]{:S(2)}) async-start(), calls=%async_computation.2 | async-start | bytes 2621440 | tf_op jit(solution)/shard_map/all_gather | solution.py:77
  77.8 132.0 %reduce-scatter.5.cloned.1.call-start = ((), (), s32[]{:S(2)}) async-start(), calls=%async_computation.5 | async-start | bytes 5242880 | tf_op jit(solution)/shard_map/reduce_scatter | solution.py:93
Sparse Core Ops, SparseCore 0:
  8.9 25.2 all-gather.4
  77.2 21.5 reduce-scatter.2
  100.5 20.7 all-gather.2
  133.0 76.7 reduce-scatter.4
where the time goes:
time: 219 us; the launch traced here: 218 us
  waiting for transfers between devices  112 us (51%)
  local copies, waits for them, and re-layouts  50.1 us (23%)
  matrix products  32.2 us (15%)
  between operations  15.2 us (7%)
  blocking collectives  5.33 us (2%)
  other arithmetic  3.74 us (2%)
    reduce_scatter x1, waiting for transfers between devices, local(): lax.psum_scatter(gathered_rows, 'pool', scatter_dimension=0, tiled=True)  76.9 us
    slice x1, local copies, waits for them, and re-layouts, local_attention(): key_all = key_value_cache[:, :, 0]  32.6 us
    reduce_scatter x1, waiting for transfers between devices, local(): lax.psum_scatter(partial_value, 'pool', scatter_dimension=1, tiled=True)  19.7 us
    squeeze x1, local copies, waits for them, and re-layouts, local_attention(): value_all = key_value_cache[:, :, 1]  15.5 us
    all_gather x1, waiting for transfers between devices, local(): att_piece = lax.all_gather(attended, 'tensor', axis=0, tiled=True)  13.7 us
    dot_general x1, matrix products, local(): jnp.dot(att_piece, output_weight, preferred_element_type=jnp.float32)  11.6 us
    dot_general x2, matrix products, local_attention(): jnp.einsum('rgd,rjd->rgj', q_rows, key_rows, preferred_element_type=jnp.f...  8.88 us
    dot_general x2, matrix products, local_attention(): jnp.einsum('rgj,rjd->rgd', weights, value_rows, preferred_element_type=jn...  6.94 us
  transfers between devices with their start and end apart: 4, of which 3 were waited for; matrix products, arithmetic and copies ran while one was open for 32% of the time, Pallas kernels for 0%

commit v1 on v0

--- a/solution.py
+++ b/solution.py
@@ -1,47 +1,73 @@
+import functools
 import math
 
 import jax
 import jax.numpy as jnp
 from jax import lax
+from jax.experimental import pallas as pl
+from jax.experimental.pallas import tpu as pltpu
 from jax.sharding import PartitionSpec as P
 
 H = 64
 KVH = 8
 HD = 128
 BLK = 128
-
+GROUP = H // KVH
 
 adapter_scale = 2.0
 
 
+def attend_row(q, kv, length):
+    heads = q.shape[0]
+    local_kv = heads // GROUP
+    owner = lax.broadcasted_iota(jnp.int32, (heads, HD), 0) // GROUP
+    wide = jnp.concatenate(
+        [jnp.where(owner == k, q, jnp.zeros_like(q)) for k in range(local_kv)], axis=1
+    )
+    scores = lax.dot_general(
+        wide, kv, (((1,), (1,)), ((), ())), preferred_element_type=jnp.float32
+    ) * (1.0 / math.sqrt(HD))
+    column = lax.broadcasted_iota(jnp.int32, scores.shape, 1)
+    visible = (column % 2 == 0) & (column < 2 * length)
+    scores = jnp.where(visible, scores, -1e30)
+    expo = jnp.where(visible, jnp.exp(scores - jnp.max(scores, axis=1, keepdims=True)), 0.0)
+    totals = jnp.sum(expo, axis=1, keepdims=True)
+    weights = pltpu.roll(expo, 1, 1).astype(jnp.bfloat16)
+    mixed = jnp.dot(weights, kv, preferred_element_type=jnp.float32)
+    picked = mixed[:, :HD]
+    for k in range(1, local_kv):
+        picked = jnp.where(owner == k, mixed[:, k * HD : (k + 1) * HD], picked)
+    return (picked / totals).astype(jnp.bfloat16)
+
+
+def attention_kernel(step_rows, lengths, q_ref, kv_ref, o_ref):
+    base = pl.program_id(0) * step_rows
+    positions, _, width = kv_ref.shape[1:]
+    for r in range(step_rows):
+        kv = kv_ref[r].reshape(positions * 2, width)
+        o_ref[r] = attend_row(q_ref[r], kv, lengths[base + r])
+
+
 def local_attention(queries, key_value_cache, cache_lengths):
-    row_count, feat_width = queries.shape
-    positions = key_value_cache.shape[1]
-    group_size = H // KVH
-    local_kv = key_value_cache.shape[3] // HD
-    key_all = key_value_cache[:, :, 0]
-    value_all = key_value_cache[:, :, 1]
-    visible = (jnp.arange(positions, dtype=jnp.int32)[None, :] < cache_lengths[:, None])[:, None, :]
-    outputs = []
-    for head in range(local_kv):
-        q_rows = queries[:, head * group_size * HD : (head + 1) * group_size * HD].reshape(
-            row_count, group_size, HD
-        )
-        key_rows = key_all[:, :, head * HD : (head + 1) * HD]
-        value_rows = value_all[:, :, head * HD : (head + 1) * HD]
-        scores = jnp.einsum(
-            "rgd,rjd->rgj", q_rows, key_rows, preferred_element_type=jnp.float32
-        ) * (1.0 / math.sqrt(HD))
-        row_max = jnp.max(jnp.where(visible, scores, -1e30), axis=-1)
-        expo_terms = jnp.where(visible, jnp.exp(scores - row_max[..., None]), 0.0)
-        totals = jnp.sum(expo_terms, axis=-1)
-        weights = expo_terms.astype(jnp.bfloat16)
-        mixed_rows = (
-            jnp.einsum("rgj,rjd->rgd", weights, value_rows, preferred_element_type=jnp.float32)
-            / totals[..., None]
-        )
-        outputs.append(mixed_rows.reshape(row_count, group_size * HD))
-    return jnp.concatenate(outputs, axis=1).astype(jnp.bfloat16)
+    rows, width = queries.shape
+    heads = width // HD
+    positions, _, kv_width = key_value_cache.shape[1:]
+    step = 8
+    out = pl.pallas_call(
+        functools.partial(attention_kernel, step),
+        grid_spec=pltpu.PrefetchScalarGridSpec(
+            num_scalar_prefetch=1,
+            grid=(rows // step,),
+            in_specs=[
+                pl.BlockSpec((step, heads, HD), lambda i, n: (i, 0, 0)),
+                pl.BlockSpec((step, positions, 2, kv_width), lambda i, n: (i, 0, 0, 0)),
+            ],
+            out_specs=pl.BlockSpec((step, heads, HD), lambda i, n: (i, 0, 0)),
+        ),
+        out_shape=jax.ShapeDtypeStruct((rows, heads, HD), jnp.bfloat16),
+        compiler_params=pltpu.CompilerParams(vmem_limit_bytes=40 * 1024 * 1024),
+    )(cache_lengths, queries.reshape(rows, heads, HD), key_value_cache)
+    return out.reshape(rows, width)
 
 
 def local(
@@ -90,8 +116,8 @@
     )
     expand_rows = expand_rows.reshape(piece_rows, output_columns)
     gathered_rows = base_output + adapter_scale * expand_rows
-    return lax.psum_scatter(gathered_rows, "pool", scatter_dimension=0, tiled=True).astype(
-        jnp.bfloat16
+    return lax.psum_scatter(
+        gathered_rows.astype(jnp.bfloat16), "pool", scatter_dimension=0, tiled=True
     )
 
 

time: 219 us -> 168 us (0.77)
  Pallas kernels: 0 us -> 47.5 us
  local copies, waits for them, and re-layouts: 50.1 us -> 5.18 us
  waiting for transfers between devices: 112 us -> 78.1 us
  matrix products: 32.2 us -> 15.6 us
  other arithmetic: 3.74 us -> 0.73 us
    pallas_call x0 -> x1, Pallas kernels: none -> 47.5 us  [local_attention(): pl.pallas_call(functools.partial(attention_kernel, step), grid_spec=pltpu...]
    reduce_scatter x1, waiting for transfers between devices: 76.9 us -> 44 us  [local(): lax.psum_scatter(gathered_rows.astype(jnp.bfloat16), 'pool', scatter_dime...]
    slice x1 -> x0, local copies, waits for them, and re-layouts: 32.6 us -> none  [local_attention(): key_all = key_value_cache[:, :, 0]]
    dot_general x4 -> x0, matrix products: 15.8 us -> none  [the longest x2 8.88 us: local_attention(): jnp.einsum('rgd,rjd->rgj', q_rows, key_rows, preferred_element_type=jnp.f...]
    squeeze x1 -> x0, local copies, waits for them, and re-layouts: 15.5 us -> none  [local_attention(): value_all = key_value_cache[:, :, 1]]
    unnamed x14 -> x8, local copies, waits for them, and re-layouts: 0.19 us -> 2.74 us
  transfers between devices with their start and end apart: 4 -> 4, of which waited for: 3 -> 3; matrix products, arithmetic and copies ran while one was open for 32% -> 5% of each run, Pallas kernels for 0% -> 28%
where the time goes in v1:
time: 168 us
  waiting for transfers between devices  78.1 us (46%)
  Pallas kernels  47.5 us (28%)
  matrix products  15.6 us (9%)
  between operations  15.1 us (9%)
  local copies, waits for them, and re-layouts  5.18 us (3%)
  blocking collectives  5.15 us (3%)
    pallas_call x1, Pallas kernels, local_attention(): pl.pallas_call(functools.partial(attention_kernel, step), grid_spec=pltpu...  47.5 us
    reduce_scatter x1, waiting for transfers between devices, local(): lax.psum_scatter(gathered_rows.astype(jnp.bfloat16), 'pool', scatter_dime...  44 us
    reduce_scatter x1, waiting for transfers between devices, local(): lax.psum_scatter(partial_value, 'pool', scatter_dimension=1, tiled=True)  19.4 us
    all_gather x1, waiting for transfers between devices, local(): att_piece = lax.all_gather(attended, 'tensor', axis=0, tiled=True)  13.9 us
    dot_general x1, matrix products, local(): jnp.dot(att_piece, output_weight, preferred_element_type=jnp.float32)  11 us
    all_gather x1, blocking collectives, local(): share_piece = lax.all_gather(rank_share, 'tensor', axis=0, tiled=True)  5.15 us
  transfers between devices with their start and end apart: 4, of which 3 were waited for; matrix products, arithmetic and copies ran while one was open for 5% of the time, Pallas kernels for 28%

profile of v1, /device:TPU:0, one launch (start us, length us, event | category | flops | bytes accessed | tf_op | source)
XLA Modules:
  0.0 167.6 jit_solution(11499659992837467120)
XLA Ops:
  6.5 0.7 all-gather.5.cloned.1.call-update
  7.3 0.0 reduce-scatter.3.cloned.1.call-start
  7.3 1.2 dynamic_slice.3
  10.5 1.1 copy.12
  11.7 0.0 copy-start.1
  11.7 0.6 copy-done.1
  12.3 47.5 %shard_map.73 = bf16[128,16,128]{2,1,0:T(8,128)(2,1)S(1)} custom-call(s32[128]{0:T(128)S(1)} %copy-done.1, bf16[128,16,128]{2,1,0:T(8,128)(2,1)S(1)} %bitcast.33, bf16[128,128,2,256]{3,2,1,0:T(2,128)(2,1)} %kv_ref.1), custom_call_target="tpu_custom_call" | custom-call | tf_op jit(solution)/shard_map/pallas_call | solution.py:56
  59.9 1.9 %fusion.1 = f32[128,64]{0,1:T(8,128)} fusion(bf16[8,2048,64]{1,2,0:T(8,128)(2,1)} %all-gather.5.cloned.1.call-done, s32[]{:T(128)} %bitcast.1, pred[]{:T(512)} %bitcast, bf16[16,8,16,128]{3,2,1,0:T(8,128)(2,1)S(1)} %bitcast.31), kind=kOutput, calls=%fused_computation.6 | convolution fusion | flops 33685504 | bytes 820224 | tf_op jit(solution)/shard_map/bnd,bdr->bnr/dot_general | solution.py:91
  61.7 0.0 reduce-scatter.3.cloned.1.call-update
  61.7 0.0 all-gather.3.cloned.1.call-start
  61.8 0.9 copy.20
  62.7 0.0 all-gather.3.cloned.1.call-update
  62.8 0.0 reduce-scatter.5.cloned.1.call-start
  62.8 0.0 copy-done.2
  62.8 0.6 gather_fusion
  63.5 0.6 gather_fusion.1
  64.1 19.4 %reduce-scatter.3.cloned.1.call-done = f32[128,16]{0,1:T(8,128)} async-done(((f32[128,64]{0,1:T(8,128)}), f32[128,16]{0,1:T(8,128)}) %reduce-scatter.3.cloned.1.call-update) | async-done | bytes 8208 | tf_op jit(solution)/shard_map/reduce_scatter | solution.py:98
  83.5 0.7 convert_element_type.6
  84.2 5.2 %all_gather.11 = bf16[512,16]{0,1:T(8,128)(2,1)S(1)} all-gather(bf16[128,16]{0,1:T(8,128)(2,1)S(1)} %convert_element_type.6), channel_id=1, replica_groups=mesh['groups'=2,'tensor'=4,'pool'=4] {'tensor'}, dimensions={0}, use_global_device_ids=true | all-gather | bytes 20480 | tf_op jit(solution)/shard_map/all_gather | solution.py:104
  89.4 2.7 %convolution_multiply_fusion = f32[4,128,2048]{2,1,0:T(8,128)} fusion(bf16[4,16,2048]{2,1,0:T(8,128)(2,1)S(1)} %gather_fusion.1, pred[4]{0:T(512)(128)(4,1)S(1)} %compare_and_fusion, bf16[512,16]{0,1:T(8,128)(2,1)S(1)} %all_gather.11), kind=kOutput, calls=%fused_computation.4 | convolution fusion | flops 34734080 | bytes 4472836 | tf_op jit(solution)/shard_map/bnr,brd->bnd/dot_general | solution.py:111
  92.1 13.9 %all-gather.3.cloned.1.call-done = bf16[512,2048]{1,0:T(8,128)(2,1)} async-done(((bf16[128,2048]{1,0:T(8,128)(2,1)}), bf16[512,2048]{1,0:T(8,128)(2,1)}) %all-gather.3.cloned.1.call-update) | async-done | bytes 2097168 | tf_op jit(solution)/shard_map/all_gather | solution.py:103
  106.0 11.0 %fusion = bf16[512,2048]{1,0:T(8,128)(2,1)} fusion(f32[4,128,2048]{2,1,0:T(8,128)} %convolution_multiply_fusion, bf16[512,2048]{1,0:T(8,128)(2,1)} %all-gather.3.cloned.1.call-done, bf16[2048,2048]{1,0:T(8,128)(2,1)} %param.11), kind=kOutput, calls=%fused_computation.3 | convolution fusion | flops 4297064448 | bytes 16777216 | tf_op jit(solution)/shard_map/dot_general | solution.py:110
  117.0 0.0 reduce-scatter.5.cloned.1.call-update
  117.0 44.0 %reduce-scatter.5.cloned.1.call-done = bf16[128,2048]{1,0:T(8,128)(2,1)} async-done(((bf16[512,2048]{1,0:T(8,128)(2,1)}), bf16[128,2048]{1,0:T(8,128)(2,1)}) %reduce-scatter.5.cloned.1.call-update) | async-done | bytes 524304 | tf_op jit(solution)/shard_map/reduce_scatter | solution.py:119
  (10 shorter events, 0.0 us)
Async XLA Ops:
  6.5 57.0 %copy-start = (bf16[8,16,2048]{2,1,0:T(8,128)(2,1)S(1)}, bf16[8,16,2048]{2,1,0:T(8,128)(2,1)}, u32[]{:S(2)}) copy-start(bf16[8,16,2048]{2,1,0:T(8,128)(2,1)} %param.13) | copy-start | bytes 1572868
  6.5 53.3 %all-gather.5.cloned.1.call-start = ((), (), s32[]{:S(2)}) async-start(), calls=%async_computation.3 | async-start | bytes 2621440 | tf_op jit(solution)/shard_map/all_gather | solution.py:89
  7.3 76.2 %reduce-scatter.3.cloned.1.call-start = ((), (), s32[]{:S(2)}) async-start(), calls=%async_computation.4 | async-start | bytes 40960 | tf_op jit(solution)/shard_map/reduce_scatter | solution.py:98
  11.7 0.7 copy-start.1
  12.3 50.5 %copy-start.2 = (s32[4]{0:T(128)S(1)}, s32[4]{0:T(128)}, u32[]{:S(2)}) copy-start(s32[4]{0:T(128)} %param.10) | copy-start | bytes 52
  61.7 44.2 %all-gather.3.cloned.1.call-start = ((), (), s32[]{:S(2)}) async-start(), calls=%async_computation.2 | async-start | bytes 2621440 | tf_op jit(solution)/shard_map/all_gather | solution.py:103
  62.8 98.3 %reduce-scatter.5.cloned.1.call-start = ((), (), s32[]{:S(2)}) async-start(), calls=%async_computation.5 | async-start | bytes 2621440 | tf_op jit(solution)/shard_map/reduce_scatter | solution.py:119
Sparse Core Ops, SparseCore 0:
  8.9 25.4 all-gather.4
  61.9 21.5 reduce-scatter.2
  85.1 20.7 all-gather.2
  117.1 43.8 reduce-scatter.4

commit v2 on v1

v2 whole, which is shorter than its diff:
```python
import functools
import math

import jax
import jax.numpy as jnp
from jax import lax
from jax.experimental import pallas as pl
from jax.experimental.pallas import tpu as pltpu
from jax.sharding import PartitionSpec as P

H = 64
KVH = 8
HD = 128
BLK = 128
GROUP = H // KVH

adapter_scale = 2.0


def attention_kernel(step_rows, lengths, q_ref, kv_ref, o_ref):
    base = pl.program_id(0) * step_rows
    positions, _, width = kv_ref.shape[1:]
    heads = q_ref.shape[1]
    local_kv = heads // GROUP
    owner = lax.broadcasted_iota(jnp.int32, (heads, HD), 0) // GROUP
    column = lax.broadcasted_iota(jnp.int32, (heads, positions * 2), 1)
    rows = range(step_rows)
    caches = [kv_ref[r].reshape(positions * 2, width) for r in rows]
    all_scores = []
    for r in rows:
        q = q_ref[r]
        wide = jnp.concatenate(
            [jnp.where(owner == k, q, jnp.zeros_like(q)) for k in range(local_kv)], axis=1
        )
        all_scores.append(
            lax.dot_general(
                wide, caches[r], (((1,), (1,)), ((), ())), preferred_element_type=jnp.float32
            )
        )
    seen = jnp.concatenate(
        [(column % 2 + jnp.where(column < 2 * lengths[base + r], 0, 2)) for r in rows], axis=0
    )
    visible = seen == 0
    scores = jnp.where(visible, jnp.concatenate(all_scores, axis=0) * (1.0 / math.sqrt(HD)), -1e30)
    expo = jnp.where(visible, jnp.exp(scores - jnp.max(scores, axis=1, keepdims=True)), 0.0)
    totals = jnp.sum(expo, axis=1, keepdims=True)
    weights = pltpu.roll(expo, 1, 1).astype(jnp.bfloat16)
    all_mixed = [
        jnp.dot(
            weights[r * heads : (r + 1) * heads], caches[r], preferred_element_type=jnp.float32
        )
        for r in rows
    ]
    for r in rows:
        mixed = all_mixed[r]
        picked = mixed[:, :HD]
        for k in range(1, local_kv):
            picked = jnp.where(owner == k, mixed[:, k * HD : (k + 1) * HD], picked)
        o_ref[r] = (picked / totals[r * heads : (r + 1) * heads]).astype(jnp.bfloat16)


def local_attention(queries, key_value_cache, cache_lengths):
    rows, width = queries.shape
    heads = width // HD
    positions, _, kv_width = key_value_cache.shape[1:]
    step = 8
    out = pl.pallas_call(
        functools.partial(attention_kernel, step),
        grid_spec=pltpu.PrefetchScalarGridSpec(
            num_scalar_prefetch=1,
            grid=(rows // step,),
            in_specs=[
                pl.BlockSpec((step, heads, HD), lambda i, n: (i, 0, 0)),
                pl.BlockSpec((step, positions, 2, kv_width), lambda i, n: (i, 0, 0, 0)),
            ],
            out_specs=pl.BlockSpec((step, heads, HD), lambda i, n: (i, 0, 0)),
        ),
        out_shape=jax.ShapeDtypeStruct((rows, heads, HD), jnp.bfloat16),
        compiler_params=pltpu.CompilerParams(vmem_limit_bytes=40 * 1024 * 1024),
    )(cache_lengths, queries.reshape(rows, heads, HD), key_value_cache)
    return out.reshape(rows, width)

MESH = pl.DeviceIdType.MESH


def project_kernel(
    nt, np_, chunks,
    att, weight, down, mask, up_mine, out,
    full, total, inbox, outbox, ups, shr, shr_in, shr_sum, shr_peer,
    att_send, att_recv, core_send, core_recv, hop_send, hop_recv,
    up_send, up_recv, one_send, one_recv, two_send, two_recv,
):
    t, p = lax.axis_index("tensor"), lax.axis_index("pool")
    block = att.shape[0]
    rows = full.shape[0]
    share = rows // np_
    wide = weight.shape[1] // chunks
    per_share = share // BLK

    def copy(src, dst, send, recv, **where):
        return pltpu.make_async_remote_copy(
            src_ref=src, dst_ref=dst, send_sem=send, recv_sem=recv,
            device_id=where, device_id_type=MESH,
        )

    def rows_of(index, size):
        return pl.ds(pl.multiple_of(index * size, size), size)

    barrier = pltpu.get_barrier_semaphore()
    for k in range(1, nt):
        pl.semaphore_signal(barrier, 1, device_id={"tensor": (t + k) % nt}, device_id_type=MESH)
    for k in range(1, np_):
        pl.semaphore_signal(barrier, 1, device_id={"pool": (p + k) % np_}, device_id_type=MESH)
    pl.semaphore_wait(barrier, nt + np_ - 2)

    other = t + 1 - 2 * (t % 2)
    own_at = full.at[rows_of(t, block)]
    sends = []
    for k in range(1, nt // 2):
        to = (t + 2 * k) % nt
        sends.append(copy(att, own_at, att_send.at[k], att_recv.at[k], tensor=to))
    sends.append(copy(att, own_at, core_send.at[0], core_recv.at[0], tensor=other))
    for k in range(1, np_):
        q = (p + k) % np_
        sends.append(
            copy(up_mine.at[pl.ds(q * per_share, per_share)], ups.at[k], up_send.at[k], up_recv.at[k], pool=q)
        )
    for each in sends:
        each.start()
    full[rows_of(t, block), :] = att[...]
    for k in range(1, nt // 2):
        came = (t + nt - 2 * k) % nt
        at = full.at[rows_of(came, block)]
        copy(att, at, att_send.at[k], att_recv.at[k], tensor=came).wait_recv()
        relay = copy(at, at, core_send.at[k], core_recv.at[k], tensor=other)
        relay.start()
        sends.append(relay)
    for k in range(nt // 2):
        at = full.at[rows_of((other + nt - 2 * k) % nt, block)]
        copy(att, at, core_send.at[k], core_recv.at[k], tensor=other).wait_recv()

    def shrink(i, carry):
        at = pl.ds(pl.multiple_of(i * BLK, BLK), BLK)
        part = jnp.dot(full[at, :], down[...], preferred_element_type=jnp.float32)
        shr[at, :] = jnp.where(mask[at, :] > 0, part, 0.0).astype(jnp.bfloat16)
        return carry

    def hop(way, q, c):
        to = p + 1 if way == 0 else p - 1
        to = jnp.clip(to, 0, np_ - 1)
        return copy(
            outbox.at[way, q, c], inbox.at[way, q, c],
            hop_send.at[way, q, c], hop_recv.at[way, q, c], pool=to,
        )

    ends = (0, np_ - 1)

    def first_hops(c):
        cols = pl.ds(pl.multiple_of(c * wide, wide), wide)
        for k in range(np_ - 1):
            for way in (0, 1):
                q = np_ - 1 - k if way == 0 else k

                @pl.when(p == ends[way])
                def _():
                    part = total[q * share : (q + 1) * share, cols]
                    outbox[way, q, c] = part.astype(jnp.bfloat16)
                    hop(way, q, c).start()

    def later_hops(c):
        cols = pl.ds(pl.multiple_of(c * wide, wide), wide)
        for k in range(np_ - 1):
            for way in (0, 1):
                q = np_ - 1 - k if way == 0 else k
                ahead = (q > p) if way == 0 else (q < p)

                @pl.when(ahead & (p != ends[way]))
                def _():
                    hop(way, q, c).wait_recv()
                    part = total[q * share : (q + 1) * share, cols]
                    part = part + inbox[way, q, c].astype(jnp.float32)
                    outbox[way, q, c] = part.astype(jnp.bfloat16)
                    hop(way, q, c).start()

        mine = rows_of(p, share)
        for way in (0, 1):

            @pl.when(p != ends[way])
            def _():
                hop(way, p, c).wait_recv()
                total[mine, cols] = total[mine, cols] + inbox[way, p, c].astype(jnp.float32)

    def one(k):
        q = (p + k) % np_
        return copy(shr.at[rows_of(q, share)], shr_in.at[k], one_send.at[k], one_recv.at[k], pool=q)

    def two(k):
        return copy(shr_sum, shr_peer.at[k], two_send.at[k], two_recv.at[k], tensor=(t + k) % nt)

    def step(c, carry):
        @pl.when(c < chunks)
        def _():
            cols = pl.ds(pl.multiple_of(c * wide, wide), wide)
            total[:, cols] = jnp.dot(
                full[...], weight[:, cols], preferred_element_type=jnp.float32
            )
            first_hops(c)

        @pl.when(c == 0)
        def _():
            lax.fori_loop(0, rows // BLK, shrink, 0)
            for k in range(1, np_):
                one(k).start()

        @pl.when(c == chunks - 1)
        def _():
            summed = shr[rows_of(p, share), :].astype(jnp.float32)
            for k in range(1, np_):
                one(k).wait_recv()
                summed = summed + shr_in[k].astype(jnp.float32)
            shr_sum[...] = summed.astype(jnp.bfloat16)
            for k in range(1, nt):
                two(k).start()

        @pl.when(c > 0)
        def _():
            later_hops(c - 1)

        return carry

    lax.fori_loop(0, chunks + 1, step, 0)

    halves = shr_sum[...].astype(jnp.float32)
    for k in range(1, nt):
        two(k).wait_recv()
        halves = halves + shr_peer[k].astype(jnp.float32)
    rank = np_ * up_mine.shape[1]
    ranks = halves[:, :rank]
    for k in range(1, halves.shape[1] // rank):
        ranks = ranks + halves[:, k * rank : (k + 1) * rank]
    shr_sum_rows = ranks.astype(jnp.bfloat16)
    ups[0] = up_mine[pl.ds(p * per_share, per_share)]
    for k in range(1, np_):
        q = (p + k) % np_
        copy(up_mine.at[pl.ds(q * per_share, per_share)], ups.at[k], up_send.at[k], up_recv.at[k], pool=q).wait_recv()
    for i in range(per_share):
        order = [ups[(p - z + np_) % np_, i].astype(jnp.float32) for z in range(np_)]
        up = jnp.concatenate(order, axis=0).astype(jnp.bfloat16)
        lines = shr_sum_rows[i * BLK : (i + 1) * BLK]
        expand = jnp.dot(lines, up, preferred_element_type=jnp.float32)
        at = pl.ds(pl.multiple_of(p * share + i * BLK, BLK), BLK)
        out[i * BLK : (i + 1) * BLK, :] = (total[at, :] + adapter_scale * expand).astype(jnp.bfloat16)

    for each in sends:
        each.wait_send()
    for k in range(1, np_):
        one(k).wait_send()
    for k in range(1, nt):
        two(k).wait_send()

    def drain(c, carry):
        for q in range(np_):
            for way in (0, 1):
                ahead = (q > p) if way == 0 else (q < p)

                @pl.when(ahead)
                def _():
                    hop(way, q, c).wait_send()

        return carry

    lax.fori_loop(0, chunks, drain, 0)


def make_local(nt, np_):
    def local(
        queries,
        key_value_cache,
        cache_lengths,
        block_adapter_slot,
        output_weight,
        adapter_down_weight,
        adapter_up_weight,
    ):
        attended = local_attention(queries, key_value_cache, cache_lengths)
        block, feat = attended.shape
        rows = block * nt
        share = rows // np_
        slots, _, rank = adapter_down_weight.shape
        columns = output_weight.shape[1]
        chunks = 4
        wide = columns // chunks
        lanes = slots * rank
        t = lax.axis_index("tensor")
        down = jnp.transpose(adapter_down_weight, (1, 0, 2)).reshape(feat, lanes)
        row_slots = jnp.repeat(block_adapter_slot, BLK)
        lane_slots = t * slots + jnp.arange(lanes, dtype=jnp.int32) // rank
        mask = (row_slots[:, None] == lane_slots[None, :]).astype(jnp.float32)
        up_mine = jnp.take(adapter_up_weight, block_adapter_slot, axis=0)
        per_share = share // BLK
        bf = jnp.bfloat16
        dma = pltpu.SemaphoreType.DMA
        boxes = (2, np_, chunks, share, wide)
        return pl.pallas_call(
            functools.partial(project_kernel, nt, np_, chunks),
            out_shape=jax.ShapeDtypeStruct((share, columns), bf),
            in_specs=[pl.BlockSpec(memory_space=pltpu.VMEM)] * 5,
            out_specs=pl.BlockSpec(memory_space=pltpu.VMEM),
            scratch_shapes=[
                pltpu.VMEM((rows, feat), bf),
                pltpu.VMEM((rows, columns), jnp.float32),
                pltpu.VMEM(boxes, bf),
                pltpu.VMEM(boxes, bf),
                pltpu.VMEM((np_, per_share, up_mine.shape[1], columns), bf),
                pltpu.VMEM((rows, lanes), bf),
                pltpu.VMEM((np_, share, lanes), bf),
                pltpu.VMEM((share, lanes), bf),
                pltpu.VMEM((nt, share, lanes), bf),
                dma((nt // 2,)), dma((nt // 2,)), dma((nt // 2,)), dma((nt // 2,)),
                dma((2, np_, chunks)), dma((2, np_, chunks)),
                dma((np_,)), dma((np_,)), dma((np_,)), dma((np_,)),
                dma((nt,)), dma((nt,)),
            ],
            compiler_params=pltpu.CompilerParams(
                collective_id=0, has_side_effects=True, vmem_limit_bytes=50 * 1024 * 1024
            ),
            cost_estimate=pl.CostEstimate(
                flops=2 * rows * feat * columns, bytes_accessed=2 * feat * columns, transcendentals=0
            ),
        )(attended, output_weight, down, mask, up_mine)

    return local


def solution(mesh):
    in_specs = (
        P(("groups", "tensor"), "pool"),
        P(("groups", "tensor"), None, None, "pool"),
        P(("groups", "tensor")),
        P("groups"),
        P("pool", "tensor"),
        P(("groups", "tensor"), "pool", None),
        P("groups", "pool", "tensor"),
    )
    out_specs = P(("groups", "pool"), "tensor")
    return jax.shard_map(make_local(mesh.shape["tensor"], mesh.shape["pool"]), mesh=mesh, in_specs=in_specs, out_specs=out_specs, check_vma=False)
```

time: 168 us -> 104 us (0.62)
  waiting for transfers between devices: 78.1 us -> 0 us
  Pallas kernels: 47.5 us -> 97.4 us
  matrix products: 15.6 us -> 0 us
  between operations: 15.1 us -> 0.07 us
  blocking collectives: 5.15 us -> 0 us
    pallas_call x0 -> x1, Pallas kernels: none -> 79.9 us  [local(): pl.pallas_call(functools.partial(project_kernel, nt, np_, chunks), out_sh...]
    reduce_scatter x2 -> x0, waiting for transfers between devices: 63.4 us -> none  [the longest x1 44 us: local(): lax.psum_scatter(gathered_rows.astype(jnp.bfloat16), 'pool', scatter_dime...]
    pallas_call x1, Pallas kernels: 47.5 us -> 17.5 us  [local_attention(): pl.pallas_call(functools.partial(attention_kernel, step), grid_spec=pltpu...]
    dot_general x3 -> x0, matrix products: 15.6 us -> none  [the longest x1 11 us: local(): jnp.dot(att_piece, output_weight, preferred_element_type=jnp.float32)]
    all_gather x2 -> x0, waiting for transfers between devices: 13.9 us -> none  [the longest x1 13.9 us: local(): att_piece = lax.all_gather(attended, 'tensor', axis=0, tiled=True)]
    all_gather x1 -> x0, blocking collectives: 5.15 us -> none  [local(): share_piece = lax.all_gather(rank_share, 'tensor', axis=0, tiled=True)]
  transfers between devices with their start and end apart: 4 -> 0, of which waited for: 3 -> 0; matrix products, arithmetic and copies ran while one was open for 5% -> 0% of each run, Pallas kernels for 28% -> 0%
where the time goes in v2:
time: 104 us; the launch traced here: 103 us
  Pallas kernels  97.4 us (94%)
  local copies, waits for them, and re-layouts  4.3 us (4%)
  other arithmetic  1.64 us (2%)
    pallas_call x1, Pallas kernels, local(): pl.pallas_call(functools.partial(project_kernel, nt, np_, chunks), out_sh...  79.9 us
    pallas_call x1, Pallas kernels, local_attention(): pl.pallas_call(functools.partial(attention_kernel, step), grid_spec=pltpu...  17.5 us
    unnamed x9, local copies, waits for them, and re-layouts  2.74 us

profile of v2, /device:TPU:0, one launch (start us, length us, event | category | flops | bytes accessed | tf_op | source)
XLA Modules:
  0.0 103.5 jit_solution(4599322076271186486)
XLA Ops:
  0.0 0.0 copy-start
  0.0 0.0 copy-start.2
  0.0 0.7 compare_and_fusion
  0.8 0.7 compare_select_fusion
  1.4 0.7 broadcast_bitcast_fusion
  2.1 0.0 copy-done
  2.2 0.6 gather_fusion
  2.7 0.1 broadcast_select_fusion.up_mine
  2.8 0.1 compare_convert_fusion.mask
  3.0 1.1 %copy.10 = bf16[16,8,16,128]{3,2,1,0:T(8,128)(2,1)S(1)} copy(bf16[16,8,16,128]{3,1,2,0:T(8,128)(2,1)} %bitcast.14) | data formatting | bytes 1048576
  4.1 0.0 copy-start.1
  4.1 0.6 copy-done.1
  4.8 17.5 %shard_map.73 = bf16[128,16,128]{2,1,0:T(8,128)(2,1)S(1)} custom-call(s32[128]{0:T(128)S(1)} %copy-done.1, bf16[128,16,128]{2,1,0:T(8,128)(2,1)S(1)} %bitcast.12, bf16[128,128,2,256]{3,2,1,0:T(2,128)(2,1)} %kv_ref.1), custom_call_target="tpu_custom_call" | custom-call | tf_op jit(solution)/shard_map/pallas_call | solution.py:67
  22.3 0.1 copy.13
  22.5 0.0 copy-done.2
  22.5 0.3 copy.9.down
  22.8 79.9 %shard_map.74 = bf16[128,2048]{1,0:T(8,128)(2,1)S(1)} custom-call(bf16[128,2048]{1,0:T(8,128)(2,1)S(1)} %bitcast.13, bf16[2048,2048]{1,0:T(8,128)(2,1)} %weight.1, bf16[2048,128]{1,0:T(8,128)(2,1)S(1)} %copy.9.down, f32[512,128]{1,0:T(8,128)S(1)} %compare_convert_fusion.mask, bf16[4,16,2048]{2,1,0:T(8,128)(2,1)S(1)} %broadcast_select_fusion.up_mine), custom_call_target="tpu_custom_call" | custom-call | flops 4294967296 | bytes 8388608 | tf_op jit(solution)/shard_map/pallas_call | solution.py:304
  102.7 0.8 copy.15
  (2 shorter events, 0.0 us)
Async XLA Ops:
  0.0 2.1 %copy-start = (bf16[8,16,2048]{2,1,0:T(8,128)(2,1)S(1)}, bf16[8,16,2048]{2,1,0:T(8,128)(2,1)}, u32[]{:S(2)}) copy-start(bf16[8,16,2048]{2,1,0:T(8,128)(2,1)} %param.13) | copy-start | bytes 1572868
  0.0 22.5 %copy-start.2 = (bf16[2,2048,64]{1,2,0:T(8,128)(2,1)S(1)}, bf16[2,2048,64]{1,2,0:T(8,128)(2,1)}, u32[]{:S(2)}) copy-start(bf16[2,2048,64]{1,2,0:T(8,128)(2,1)} %param.12) | copy-start | bytes 1572868
  4.1 0.7 copy-start.1

commit v3 on v2

--- a/solution.py
+++ b/solution.py
@@ -17,18 +17,16 @@
 adapter_scale = 2.0
 
 
-def attention_kernel(step_rows, lengths, q_ref, kv_ref, o_ref):
-    base = pl.program_id(0) * step_rows
+def attend_rows(rows, base, lengths, q_ref, kv_ref):
     positions, _, width = kv_ref.shape[1:]
     heads = q_ref.shape[1]
     local_kv = heads // GROUP
     owner = lax.broadcasted_iota(jnp.int32, (heads, HD), 0) // GROUP
     column = lax.broadcasted_iota(jnp.int32, (heads, positions * 2), 1)
-    rows = range(step_rows)
-    caches = [kv_ref[r].reshape(positions * 2, width) for r in rows]
+    caches = [kv_ref[r].reshape(positions * 2, width) for r in range(rows)]
     all_scores = []
-    for r in rows:
-        q = q_ref[r]
+    for r in range(rows):
+        q = q_ref[base + r]
         wide = jnp.concatenate(
             [jnp.where(owner == k, q, jnp.zeros_like(q)) for k in range(local_kv)], axis=1
         )
@@ -38,7 +36,7 @@
             )
         )
     seen = jnp.concatenate(
-        [(column % 2 + jnp.where(column < 2 * lengths[base + r], 0, 2)) for r in rows], axis=0
+        [(column % 2 + jnp.where(column < 2 * lengths[base + r], 0, 2)) for r in range(rows)], axis=0
     )
     visible = seen == 0
     scores = jnp.where(visible, jnp.concatenate(all_scores, axis=0) * (1.0 / math.sqrt(HD)), -1e30)
@@ -49,49 +47,32 @@
         jnp.dot(
             weights[r * heads : (r + 1) * heads], caches[r], preferred_element_type=jnp.float32
         )
-        for r in rows
+        for r in range(rows)
     ]
-    for r in rows:
+    done = []
+    for r in range(rows):
         mixed = all_mixed[r]
         picked = mixed[:, :HD]
         for k in range(1, local_kv):
             picked = jnp.where(owner == k, mixed[:, k * HD : (k + 1) * HD], picked)
-        o_ref[r] = (picked / totals[r * heads : (r + 1) * heads]).astype(jnp.bfloat16)
-
-
-def local_attention(queries, key_value_cache, cache_lengths):
-    rows, width = queries.shape
-    heads = width // HD
-    positions, _, kv_width = key_value_cache.shape[1:]
-    step = 8
-    out = pl.pallas_call(
-        functools.partial(attention_kernel, step),
-        grid_spec=pltpu.PrefetchScalarGridSpec(
-            num_scalar_prefetch=1,
-            grid=(rows // step,),
-            in_specs=[
-                pl.BlockSpec((step, heads, HD), lambda i, n: (i, 0, 0)),
-                pl.BlockSpec((step, positions, 2, kv_width), lambda i, n: (i, 0, 0, 0)),
-            ],
-            out_specs=pl.BlockSpec((step, heads, HD), lambda i, n: (i, 0, 0)),
-        ),
-        out_shape=jax.ShapeDtypeStruct((rows, heads, HD), jnp.bfloat16),
-        compiler_params=pltpu.CompilerParams(vmem_limit_bytes=40 * 1024 * 1024),
-    )(cache_lengths, queries.reshape(rows, heads, HD), key_value_cache)
-    return out.reshape(rows, width)
+        done.append((picked / totals[r * heads : (r + 1) * heads])[None])
+    return jnp.concatenate(done, axis=0)
+
 
 MESH = pl.DeviceIdType.MESH
+PIECES = 4
+STEP = 16
 
 
 def project_kernel(
     nt, np_, chunks,
-    att, weight, down, mask, up_mine, out,
-    full, total, inbox, outbox, ups, shr, shr_in, shr_sum, shr_peer,
+    lengths, queries, cache, weight_hbm, down, mask, up_mine, out,
+    kv_buf, kv_sem, weight, weight_sem, full, total, inbox, outbox, ups, shr, shr_in, shr_sum, shr_peer,
     att_send, att_recv, core_send, core_recv, hop_send, hop_recv,
     up_send, up_recv, one_send, one_recv, two_send, two_recv,
 ):
     t, p = lax.axis_index("tensor"), lax.axis_index("pool")
-    block = att.shape[0]
+    block = queries.shape[0]
     rows = full.shape[0]
     share = rows // np_
     wide = weight.shape[1] // chunks
@@ -105,6 +86,16 @@
 
     def rows_of(index, size):
         return pl.ds(pl.multiple_of(index * size, size), size)
+
+    group = kv_buf.shape[1]
+    steps = block // group // PIECES
+    piece = block // PIECES
+
+    def fetch(i):
+        return pltpu.make_async_copy(cache.at[pl.ds(i * group, group)], kv_buf.at[i % 2], kv_sem.at[i % 2])
+
+    fetch(0).start()
+    weight_copy = pltpu.make_async_copy(weight_hbm, weight, weight_sem)
 
     barrier = pltpu.get_barrier_semaphore()
     for k in range(1, nt):
@@ -114,12 +105,7 @@
     pl.semaphore_wait(barrier, nt + np_ - 2)
 
     other = t + 1 - 2 * (t % 2)
-    own_at = full.at[rows_of(t, block)]
     sends = []
-    for k in range(1, nt // 2):
-        to = (t + 2 * k) % nt
-        sends.append(copy(att, own_at, att_send.at[k], att_recv.at[k], tensor=to))
-    sends.append(copy(att, own_at, core_send.at[0], core_recv.at[0], tensor=other))
     for k in range(1, np_):
         q = (p + k) % np_
         sends.append(
@@ -127,17 +113,61 @@
         )
     for each in sends:
         each.start()
-    full[rows_of(t, block), :] = att[...]
-    for k in range(1, nt // 2):
-        came = (t + nt - 2 * k) % nt
-        at = full.at[rows_of(came, block)]
-        copy(att, at, att_send.at[k], att_recv.at[k], tensor=came).wait_recv()
-        relay = copy(at, at, core_send.at[k], core_recv.at[k], tensor=other)
-        relay.start()
-        sends.append(relay)
-    for k in range(nt // 2):
-        at = full.at[rows_of((other + nt - 2 * k) % nt, block)]
-        copy(att, at, core_send.at[k], core_recv.at[k], tensor=other).wait_recv()
+
+    def part_of(owner, j):
+        return full.at[rows_of(owner * PIECES + j, piece)]
+
+    def across(k, j):
+        at = part_of(t, j)
+        return copy(at, at, att_send.at[k, j], att_recv.at[k, j], tensor=(t + 2 * k) % nt)
+
+    def beside(k, j):
+        at = part_of((t + nt - 2 * k) % nt, j)
+        return copy(at, at, core_send.at[k, j], core_recv.at[k, j], tensor=other)
+
+    def relay(j):
+        for k in range(1, nt // 2):
+            across(k, j).wait_recv()
+            beside(k, j).start()
+
+    def attend_piece(j, carry):
+        def attend_step(n, carry):
+            i = j * steps + n
+
+            @pl.when(i + 1 < block // group)
+            def _():
+                fetch(i + 1).start()
+
+            fetch(i).wait()
+            rows_done = attend_rows(group, i * group, lengths, queries, kv_buf.at[i % 2])
+            by_head = jnp.swapaxes(rows_done, 0, 1)
+            at = rows_of(t * (block // group) + i, group)
+            for h in range(by_head.shape[0]):
+                full[at, h * HD : (h + 1) * HD] = by_head[h].astype(jnp.bfloat16)
+
+            @pl.when(i == 0)
+            def _():
+                weight_copy.start()
+
+            return carry
+
+        lax.fori_loop(0, steps, attend_step, 0)
+        for k in range(1, nt // 2):
+            across(k, j).start()
+        beside(0, j).start()
+
+        @pl.when(j > 0)
+        def _():
+            relay(j - 1)
+
+        return carry
+
+    lax.fori_loop(0, PIECES, attend_piece, 0)
+    relay(PIECES - 1)
+    weight_copy.wait()
+    for j in range(PIECES):
+        for k in range(nt // 2):
+            beside(k, j).wait_recv()
 
     def shrink(i, carry):
         at = pl.ds(pl.multiple_of(i * BLK, BLK), BLK)
@@ -253,6 +283,11 @@
 
     for each in sends:
         each.wait_send()
+    for j in range(PIECES):
+        for k in range(nt // 2):
+            beside(k, j).wait_send()
+        for k in range(1, nt // 2):
+            across(k, j).wait_send()
     for k in range(1, np_):
         one(k).wait_send()
     for k in range(1, nt):
@@ -282,13 +317,12 @@
         adapter_down_weight,
         adapter_up_weight,
     ):
-        attended = local_attention(queries, key_value_cache, cache_lengths)
-        block, feat = attended.shape
+        block, feat = queries.shape
         rows = block * nt
         share = rows // np_
         slots, _, rank = adapter_down_weight.shape
         columns = output_weight.shape[1]
-        chunks = 4
+        chunks = max(1, min(8, columns // 256))
         wide = columns // chunks
         lanes = slots * rank
         t = lax.axis_index("tensor")
@@ -304,9 +338,19 @@
         return pl.pallas_call(
             functools.partial(project_kernel, nt, np_, chunks),
             out_shape=jax.ShapeDtypeStruct((share, columns), bf),
-            in_specs=[pl.BlockSpec(memory_space=pltpu.VMEM)] * 5,
+            in_specs=[
+                pl.BlockSpec(memory_space=pltpu.SMEM),
+                pl.BlockSpec(memory_space=pltpu.VMEM),
+                pl.BlockSpec(memory_space=pl.ANY),
+                pl.BlockSpec(memory_space=pl.ANY),
+            ]
+            + [pl.BlockSpec(memory_space=pltpu.VMEM)] * 3,
             out_specs=pl.BlockSpec(memory_space=pltpu.VMEM),
             scratch_shapes=[
+                pltpu.VMEM((2, STEP) + key_value_cache.shape[1:], bf),
+                dma((2,)),
+                pltpu.VMEM((feat, columns), bf),
+                dma,
                 pltpu.VMEM((rows, feat), bf),
                 pltpu.VMEM((rows, columns), jnp.float32),
                 pltpu.VMEM(boxes, bf),
@@ -316,7 +360,7 @@
                 pltpu.VMEM((np_, share, lanes), bf),
                 pltpu.VMEM((share, lanes), bf),
                 pltpu.VMEM((nt, share, lanes), bf),
-                dma((nt // 2,)), dma((nt // 2,)), dma((nt // 2,)), dma((nt // 2,)),
+                dma((nt // 2, PIECES)), dma((nt // 2, PIECES)), dma((nt // 2, PIECES)), dma((nt // 2, PIECES)),
                 dma((2, np_, chunks)), dma((2, np_, chunks)),
                 dma((np_,)), dma((np_,)), dma((np_,)), dma((np_,)),
                 dma((nt,)), dma((nt,)),
@@ -327,7 +371,10 @@
             cost_estimate=pl.CostEstimate(
                 flops=2 * rows * feat * columns, bytes_accessed=2 * feat * columns, transcendentals=0
             ),
-        )(attended, output_weight, down, mask, up_mine)
+        )(
+            cache_lengths, queries.reshape(block, feat // HD, HD), key_value_cache, output_weight,
+            down, mask, up_mine,
+        )
 
     return local
 

time: 104 us -> 106 us (1.019)
  Pallas kernels: 97.4 us -> 99.1 us
    pallas_call x1, Pallas kernels: 79.9 us -> 99.1 us  [local(): pl.pallas_call(functools.partial(project_kernel, nt, np_, chunks), out_sh...]
    pallas_call x1 -> x0, Pallas kernels: 17.5 us -> none  [local_attention(): pl.pallas_call(functools.partial(attention_kernel, step), grid_spec=pltpu...]
    unnamed x9 -> x6, local copies, waits for them, and re-layouts: 2.74 us -> 2.6 us
where the time goes in v3:
time: 106 us
  Pallas kernels  99.1 us (93%)
  local copies, waits for them, and re-layouts  5.2 us (5%)
  other arithmetic  1.61 us (2%)
    pallas_call x1, Pallas kernels, local(): pl.pallas_call(functools.partial(project_kernel, nt, np_, chunks), out_sh...  99.1 us
    unnamed x6, local copies, waits for them, and re-layouts  2.6 us

profile of v3, /device:TPU:0, one launch (start us, length us, event | category | flops | bytes accessed | tf_op | source)
XLA Modules:
  0.0 106.0 jit_solution(2807535296205367722)
XLA Ops:
  0.0 0.0 copy-start
  0.0 0.7 compare_and_fusion
  0.7 0.7 compare_select_fusion
  1.4 0.7 broadcast_bitcast_fusion
  2.1 0.0 copy-done
  2.1 0.6 gather_fusion
  2.7 0.1 broadcast_select_fusion.up_mine
  2.8 0.1 compare_convert_fusion.mask
  2.9 1.1 %copy.10 = bf16[16,8,16,128]{3,2,1,0:T(8,128)(2,1)S(1)} copy(bf16[16,8,16,128]{3,1,2,0:T(8,128)(2,1)} %bitcast.8) | data formatting | bytes 1048576
  4.1 1.3 %copy.9.down = bf16[2048,128]{1,0:T(8,128)(2,1)S(1)} copy(bf16[2048,128]{0,1:T(8,128)(2,1)} %bitcast.9) | data formatting | bytes 1048576 | tf_op jit(solution)/shard_map/reshape | solution.py:329
  5.4 0.0 copy-start.1
  5.4 0.6 copy-done.1
  6.1 99.1 %shard_map.73 = bf16[128,2048]{1,0:T(8,128)(2,1)S(1)} custom-call(s32[128]{0:T(128)S(1)} %copy-done.1, bf16[128,16,128]{2,1,0:T(8,128)(2,1)S(1)} %bitcast.7, bf16[128,128,2,256]{3,2,1,0:T(2,128)(2,1)} %cache.1, bf16[2048,2048]{1,0:T(8,128)(2,1)} %weight_hbm.1, bf16[2048,128]{1,0:T(8,128)(2,1)S(1)} %copy.9.down, f32[512,128]{1,0:T(8,128)S(1)} %compare_convert_fusion.mask, ...), custom_call_target="tpu_custom_call" | custom-call | flops 4294967296 | bytes 8388608 | tf_op jit(solution)/shard_map/pallas_call | solution.py:338
  105.2 0.8 copy.12
  (2 shorter events, 0.0 us)
Async XLA Ops:
  0.0 2.1 %copy-start = (bf16[8,16,2048]{2,1,0:T(8,128)(2,1)S(1)}, bf16[8,16,2048]{2,1,0:T(8,128)(2,1)}, u32[]{:S(2)}) copy-start(bf16[8,16,2048]{2,1,0:T(8,128)(2,1)} %param.13) | copy-start | bytes 1572868
  5.4 0.7 copy-start.1

commit v4 on v3

--- a/solution.py
+++ b/solution.py
@@ -185,40 +185,34 @@
 
     ends = (0, np_ - 1)
 
-    def first_hops(c):
-        cols = pl.ds(pl.multiple_of(c * wide, wide), wide)
-        for k in range(np_ - 1):
-            for way in (0, 1):
-                q = np_ - 1 - k if way == 0 else k
-
-                @pl.when(p == ends[way])
-                def _():
-                    part = total[q * share : (q + 1) * share, cols]
-                    outbox[way, q, c] = part.astype(jnp.bfloat16)
-                    hop(way, q, c).start()
-
-    def later_hops(c):
-        cols = pl.ds(pl.multiple_of(c * wide, wide), wide)
-        for k in range(np_ - 1):
+    def hops(c):
+        behind = (p, np_ - 1 - p)
+        for k in range(np_):
             for way in (0, 1):
                 q = np_ - 1 - k if way == 0 else k
                 ahead = (q > p) if way == 0 else (q < p)
-
-                @pl.when(ahead & (p != ends[way]))
+                at = c - behind[way]
+                inside = (at >= 0) & (at < chunks)
+                d = jnp.clip(at, 0, chunks - 1)
+                cols = pl.ds(pl.multiple_of(d * wide, wide), wide)
+                lines = slice(q * share, (q + 1) * share)
+
+                @pl.when(inside & ahead & (behind[way] == 0))
                 def _():
-                    hop(way, q, c).wait_recv()
-                    part = total[q * share : (q + 1) * share, cols]
-                    part = part + inbox[way, q, c].astype(jnp.float32)
-                    outbox[way, q, c] = part.astype(jnp.bfloat16)
-                    hop(way, q, c).start()
-
-        mine = rows_of(p, share)
-        for way in (0, 1):
-
-            @pl.when(p != ends[way])
-            def _():
-                hop(way, p, c).wait_recv()
-                total[mine, cols] = total[mine, cols] + inbox[way, p, c].astype(jnp.float32)
+                    outbox[way, q, d] = total[lines, cols].astype(jnp.bfloat16)
+                    hop(way, q, d).start()
+
+                @pl.when(inside & ahead & (behind[way] > 0))
+                def _():
+                    hop(way, q, d).wait_recv()
+                    part = total[lines, cols] + inbox[way, q, d].astype(jnp.float32)
+                    outbox[way, q, d] = part.astype(jnp.bfloat16)
+                    hop(way, q, d).start()
+
+                @pl.when(inside & (p == q) & (behind[way] > 0))
+                def _():
+                    hop(way, q, d).wait_recv()
+                    total[lines, cols] = total[lines, cols] + inbox[way, q, d].astype(jnp.float32)
 
     def one(k):
         q = (p + k) % np_
@@ -234,7 +228,8 @@
             total[:, cols] = jnp.dot(
                 full[...], weight[:, cols], preferred_element_type=jnp.float32
             )
-            first_hops(c)
+
+        hops(c)
 
         @pl.when(c == 0)
         def _():
@@ -252,13 +247,9 @@
             for k in range(1, nt):
                 two(k).start()
 
-        @pl.when(c > 0)
-        def _():
-            later_hops(c - 1)
-
         return carry
 
-    lax.fori_loop(0, chunks + 1, step, 0)
+    lax.fori_loop(0, chunks + np_ - 1, step, 0)
 
     halves = shr_sum[...].astype(jnp.float32)
     for k in range(1, nt):

time: 106 us -> 76.5 us (0.72)
  Pallas kernels: 99.1 us -> 69.3 us
    pallas_call x1, Pallas kernels: 99.1 us -> 69.3 us  [local(): pl.pallas_call(functools.partial(project_kernel, nt, np_, chunks), out_sh...]
where the time goes in v4:
time: 76.5 us; the launch traced here: 76.2 us
  Pallas kernels  69.3 us (91%)
  local copies, waits for them, and re-layouts  5.2 us (7%)
  other arithmetic  1.61 us (2%)
    pallas_call x1, Pallas kernels, local(): pl.pallas_call(functools.partial(project_kernel, nt, np_, chunks), out_sh...  69.3 us
    unnamed x6, local copies, waits for them, and re-layouts  2.6 us

profile of v4, /device:TPU:0, one launch (start us, length us, event | category | flops | bytes accessed | tf_op | source)
XLA Modules:
  0.0 76.2 jit_solution(3043634621124922687)
XLA Ops:
  0.0 0.0 copy-start
  0.0 0.7 compare_and_fusion
  0.7 0.7 compare_select_fusion
  1.4 0.7 broadcast_bitcast_fusion
  2.1 0.0 copy-done
  2.1 0.6 gather_fusion
  2.7 0.1 broadcast_select_fusion.up_mine
  2.8 0.1 compare_convert_fusion.mask
  2.9 1.1 %copy.10 = bf16[16,8,16,128]{3,2,1,0:T(8,128)(2,1)S(1)} copy(bf16[16,8,16,128]{3,1,2,0:T(8,128)(2,1)} %bitcast.8) | data formatting | bytes 1048576
  4.1 1.3 %copy.9.down = bf16[2048,128]{1,0:T(8,128)(2,1)S(1)} copy(bf16[2048,128]{0,1:T(8,128)(2,1)} %bitcast.9) | data formatting | bytes 1048576 | tf_op jit(solution)/shard_map/reshape | solution.py:320
  5.4 0.0 copy-start.1
  5.4 0.6 copy-done.1
  6.1 69.3 %shard_map.73 = bf16[128,2048]{1,0:T(8,128)(2,1)S(1)} custom-call(s32[128]{0:T(128)S(1)} %copy-done.1, bf16[128,16,128]{2,1,0:T(8,128)(2,1)S(1)} %bitcast.7, bf16[128,128,2,256]{3,2,1,0:T(2,128)(2,1)} %cache.1, bf16[2048,2048]{1,0:T(8,128)(2,1)} %weight_hbm.1, bf16[2048,128]{1,0:T(8,128)(2,1)S(1)} %copy.9.down, f32[512,128]{1,0:T(8,128)S(1)} %compare_convert_fusion.mask, ...), custom_call_target="tpu_custom_call" | custom-call | flops 4294967296 | bytes 8388608 | tf_op jit(solution)/shard_map/pallas_call | solution.py:329
  75.4 0.8 %copy.12 = bf16[128,2048]{1,0:T(8,128)(2,1)} copy(bf16[128,2048]{1,0:T(8,128)(2,1)S(1)} %shard_map.73) | data formatting | bytes 1048576
  (2 shorter events, 0.0 us)
Async XLA Ops:
  0.0 2.1 %copy-start = (bf16[8,16,2048]{2,1,0:T(8,128)(2,1)S(1)}, bf16[8,16,2048]{2,1,0:T(8,128)(2,1)}, u32[]{:S(2)}) copy-start(bf16[8,16,2048]{2,1,0:T(8,128)(2,1)} %param.13) | copy-start | bytes 1572868
  5.4 0.7 copy-start.1

commit v5 on v4

--- a/solution.py
+++ b/solution.py
@@ -60,7 +60,7 @@
 
 
 MESH = pl.DeviceIdType.MESH
-PIECES = 4
+PIECES = 2
 STEP = 16
 
 
@@ -77,6 +77,8 @@
     share = rows // np_
     wide = weight.shape[1] // chunks
     per_share = share // BLK
+    half = rows // PIECES
+    part_share = share // PIECES
 
     def copy(src, dst, send, recv, **where):
         return pltpu.make_async_remote_copy(
@@ -115,7 +117,7 @@
         each.start()
 
     def part_of(owner, j):
-        return full.at[rows_of(owner * PIECES + j, piece)]
+        return full.at[rows_of(j * nt + owner, piece)]
 
     def across(k, j):
         at = part_of(t, j)
@@ -130,50 +132,45 @@
             across(k, j).wait_recv()
             beside(k, j).start()
 
-    def attend_piece(j, carry):
-        def attend_step(n, carry):
-            i = j * steps + n
-
-            @pl.when(i + 1 < block // group)
-            def _():
-                fetch(i + 1).start()
-
-            fetch(i).wait()
-            rows_done = attend_rows(group, i * group, lengths, queries, kv_buf.at[i % 2])
-            by_head = jnp.swapaxes(rows_done, 0, 1)
-            at = rows_of(t * (block // group) + i, group)
-            for h in range(by_head.shape[0]):
-                full[at, h * HD : (h + 1) * HD] = by_head[h].astype(jnp.bfloat16)
-
-            @pl.when(i == 0)
-            def _():
-                weight_copy.start()
-
-            return carry
-
-        lax.fori_loop(0, steps, attend_step, 0)
+    def attend_step(i, carry):
+        @pl.when(i + 1 < block // group)
+        def _():
+            fetch(i + 1).start()
+
+        fetch(i).wait()
+        rows_done = attend_rows(group, i * group, lengths, queries, kv_buf.at[i % 2])
+        by_head = jnp.swapaxes(rows_done, 0, 1)
+        at = rows_of(((i // steps) * nt + t) * steps + i % steps, group)
+        for h in range(by_head.shape[0]):
+            full[at, h * HD : (h + 1) * HD] = by_head[h].astype(jnp.bfloat16)
+
+        @pl.when(i == 0)
+        def _():
+            weight_copy.start()
+
+        return carry
+
+    def send_piece(j):
         for k in range(1, nt // 2):
             across(k, j).start()
         beside(0, j).start()
 
-        @pl.when(j > 0)
-        def _():
-            relay(j - 1)
-
-        return carry
-
-    lax.fori_loop(0, PIECES, attend_piece, 0)
-    relay(PIECES - 1)
-    weight_copy.wait()
-    for j in range(PIECES):
+    def wait_piece(j):
         for k in range(nt // 2):
             beside(k, j).wait_recv()
 
-    def shrink(i, carry):
-        at = pl.ds(pl.multiple_of(i * BLK, BLK), BLK)
+    lax.fori_loop(0, steps, attend_step, 0)
+    send_piece(0)
+    relay(0)
+    weight_copy.wait()
+    wait_piece(0)
+
+    def shrink(j):
+        at = slice(j * half, (j + 1) * half)
         part = jnp.dot(full[at, :], down[...], preferred_element_type=jnp.float32)
-        shr[at, :] = jnp.where(mask[at, :] > 0, part, 0.0).astype(jnp.bfloat16)
-        return carry
+        part = jnp.where(mask[at, :] > 0, part, 0.0).astype(jnp.bfloat16)
+        for q in range(np_):
+            shr[q, j * part_share : (j + 1) * part_share, :] = part[q * part_share : (q + 1) * part_share]
 
     def hop(way, q, c):
         to = p + 1 if way == 0 else p - 1
@@ -183,7 +180,8 @@
             hop_send.at[way, q, c], hop_recv.at[way, q, c], pool=to,
         )
 
-    ends = (0, np_ - 1)
+    turns = PIECES * chunks
+    busy = min(2, chunks)
 
     def hops(c):
         behind = (p, np_ - 1 - p)
@@ -192,10 +190,10 @@
                 q = np_ - 1 - k if way == 0 else k
                 ahead = (q > p) if way == 0 else (q < p)
                 at = c - behind[way]
-                inside = (at >= 0) & (at < chunks)
-                d = jnp.clip(at, 0, chunks - 1)
-                cols = pl.ds(pl.multiple_of(d * wide, wide), wide)
-                lines = slice(q * share, (q + 1) * share)
+                inside = (at >= 0) & (at < turns)
+                d = jnp.clip(at, 0, turns - 1)
+                cols = pl.ds(pl.multiple_of(d % chunks * wide, wide), wide)
+                lines = rows_of(d // chunks * np_ + q, part_share)
 
                 @pl.when(inside & ahead & (behind[way] == 0))
                 def _():
@@ -216,30 +214,49 @@
 
     def one(k):
         q = (p + k) % np_
-        return copy(shr.at[rows_of(q, share)], shr_in.at[k], one_send.at[k], one_recv.at[k], pool=q)
+        return copy(shr.at[q], shr_in.at[k], one_send.at[k], one_recv.at[k], pool=q)
 
     def two(k):
         return copy(shr_sum, shr_peer.at[k], two_send.at[k], two_recv.at[k], tensor=(t + k) % nt)
 
     def step(c, carry):
-        @pl.when(c < chunks)
-        def _():
-            cols = pl.ds(pl.multiple_of(c * wide, wide), wide)
-            total[:, cols] = jnp.dot(
-                full[...], weight[:, cols], preferred_element_type=jnp.float32
+        @pl.when(c == chunks)
+        def _():
+            wait_piece(1)
+
+        @pl.when(c < turns)
+        def _():
+            cols = pl.ds(pl.multiple_of(c % chunks * wide, wide), wide)
+            lines = rows_of(c // chunks, half)
+            total[lines, cols] = jnp.dot(
+                full[lines, :], weight[:, cols], preferred_element_type=jnp.float32
             )
 
         hops(c)
 
-        @pl.when(c == 0)
-        def _():
-            lax.fori_loop(0, rows // BLK, shrink, 0)
+        @pl.when(c < busy)
+        def _():
+            each = steps // busy
+            lax.fori_loop(steps + c * each, steps + (c + 1) * each, attend_step, 0)
+
+        @pl.when(c == busy - 1)
+        def _():
+            send_piece(1)
+
+        @pl.when(c == chunks - 1)
+        def _():
+            shrink(0)
+            relay(1)
+
+        @pl.when(c == chunks)
+        def _():
+            shrink(1)
             for k in range(1, np_):
                 one(k).start()
 
-        @pl.when(c == chunks - 1)
-        def _():
-            summed = shr[rows_of(p, share), :].astype(jnp.float32)
+        @pl.when(c == turns)
+        def _():
+            summed = shr[p].astype(jnp.float32)
             for k in range(1, np_):
                 one(k).wait_recv()
                 summed = summed + shr_in[k].astype(jnp.float32)
@@ -249,7 +266,7 @@
 
         return carry
 
-    lax.fori_loop(0, chunks + np_ - 1, step, 0)
+    lax.fori_loop(0, turns + np_ - 1, step, 0)
 
     halves = shr_sum[...].astype(jnp.float32)
     for k in range(1, nt):
@@ -267,10 +284,14 @@
     for i in range(per_share):
         order = [ups[(p - z + np_) % np_, i].astype(jnp.float32) for z in range(np_)]
         up = jnp.concatenate(order, axis=0).astype(jnp.bfloat16)
-        lines = shr_sum_rows[i * BLK : (i + 1) * BLK]
-        expand = jnp.dot(lines, up, preferred_element_type=jnp.float32)
-        at = pl.ds(pl.multiple_of(p * share + i * BLK, BLK), BLK)
-        out[i * BLK : (i + 1) * BLK, :] = (total[at, :] + adapter_scale * expand).astype(jnp.bfloat16)
+        for j in range(PIECES):
+            first = j * part_share + i * piece
+            expand = jnp.dot(
+                shr_sum_rows[first : first + piece], up, preferred_element_type=jnp.float32
+            )
+            at = rows_of(j * (half // piece) + p * per_share + i, piece)
+            to = i * BLK + j * piece
+            out[to : to + piece, :] = (total[at, :] + adapter_scale * expand).astype(jnp.bfloat16)
 
     for each in sends:
         each.wait_send()
@@ -295,7 +316,7 @@
 
         return carry
 
-    lax.fori_loop(0, chunks, drain, 0)
+    lax.fori_loop(0, turns, drain, 0)
 
 
 def make_local(nt, np_):
@@ -313,19 +334,19 @@
         share = rows // np_
         slots, _, rank = adapter_down_weight.shape
         columns = output_weight.shape[1]
-        chunks = max(1, min(8, columns // 256))
+        chunks = max(1, min(4, columns // 512))
         wide = columns // chunks
         lanes = slots * rank
         t = lax.axis_index("tensor")
         down = jnp.transpose(adapter_down_weight, (1, 0, 2)).reshape(feat, lanes)
-        row_slots = jnp.repeat(block_adapter_slot, BLK)
+        row_slots = jnp.tile(jnp.repeat(block_adapter_slot, BLK // PIECES), PIECES)
         lane_slots = t * slots + jnp.arange(lanes, dtype=jnp.int32) // rank
         mask = (row_slots[:, None] == lane_slots[None, :]).astype(jnp.float32)
         up_mine = jnp.take(adapter_up_weight, block_adapter_slot, axis=0)
         per_share = share // BLK
         bf = jnp.bfloat16
         dma = pltpu.SemaphoreType.DMA
-        boxes = (2, np_, chunks, share, wide)
+        boxes = (2, np_, PIECES * chunks, share // PIECES, wide)
         return pl.pallas_call(
             functools.partial(project_kernel, nt, np_, chunks),
             out_shape=jax.ShapeDtypeStruct((share, columns), bf),
@@ -347,12 +368,12 @@
                 pltpu.VMEM(boxes, bf),
                 pltpu.VMEM(boxes, bf),
                 pltpu.VMEM((np_, per_share, up_mine.shape[1], columns), bf),
-                pltpu.VMEM((rows, lanes), bf),
+                pltpu.VMEM((np_, share, lanes), bf),
                 pltpu.VMEM((np_, share, lanes), bf),
                 pltpu.VMEM((share, lanes), bf),
                 pltpu.VMEM((nt, share, lanes), bf),
                 dma((nt // 2, PIECES)), dma((nt // 2, PIECES)), dma((nt // 2, PIECES)), dma((nt // 2, PIECES)),
-                dma((2, np_, chunks)), dma((2, np_, chunks)),
+                dma((2, np_, PIECES * chunks)), dma((2, np_, PIECES * chunks)),
                 dma((np_,)), dma((np_,)), dma((np_,)), dma((np_,)),
                 dma((nt,)), dma((nt,)),
             ],

time: 76.5 us -> 73.9 us (0.966)
  Pallas kernels: 69.3 us -> 66.7 us
    pallas_call x1, Pallas kernels: 69.3 us -> 66.7 us  [local(): pl.pallas_call(functools.partial(project_kernel, nt, np_, chunks), out_sh...]
    unnamed x6 -> x8, local copies, waits for them, and re-layouts: 2.6 us -> 2.61 us
where the time goes in v5:
time: 73.9 us; the launch traced here: 73.6 us
  Pallas kernels  66.7 us (90%)
  local copies, waits for them, and re-layouts  5.29 us (7%)
  other arithmetic  1.61 us (2%)
    pallas_call x1, Pallas kernels, local(): pl.pallas_call(functools.partial(project_kernel, nt, np_, chunks), out_sh...  66.7 us
    unnamed x8, local copies, waits for them, and re-layouts  2.61 us

profile of v5, /device:TPU:0, one launch (start us, length us, event | category | flops | bytes accessed | tf_op | source)
XLA Modules:
  0.0 73.6 jit_solution(17534308194994179538)
XLA Ops:
  0.0 0.0 copy-start
  0.0 0.7 compare_and_fusion
  0.7 0.7 compare_select_fusion
  1.4 0.7 broadcast_in_dim.16
  2.1 0.1 tile.7
  2.2 0.0 copy-done
  2.2 0.6 gather_fusion
  2.8 0.1 broadcast_select_fusion.up_mine
  2.9 0.1 compare_convert_fusion.mask
  3.0 1.1 %copy.10 = bf16[16,8,16,128]{3,2,1,0:T(8,128)(2,1)S(1)} copy(bf16[16,8,16,128]{3,1,2,0:T(8,128)(2,1)} %bitcast.9) | data formatting | bytes 1048576
  4.2 1.3 %copy.9.down = bf16[2048,128]{1,0:T(8,128)(2,1)S(1)} copy(bf16[2048,128]{0,1:T(8,128)(2,1)} %bitcast.10) | data formatting | bytes 1048576 | tf_op jit(solution)/shard_map/reshape | solution.py:341
  5.5 0.0 copy-start.1
  5.5 0.6 copy-done.1
  6.2 66.7 %shard_map.73 = bf16[128,2048]{1,0:T(8,128)(2,1)S(1)} custom-call(s32[128]{0:T(128)S(1)} %copy-done.1, bf16[128,16,128]{2,1,0:T(8,128)(2,1)S(1)} %bitcast.8, bf16[128,128,2,256]{3,2,1,0:T(2,128)(2,1)} %cache.1, bf16[2048,2048]{1,0:T(8,128)(2,1)} %weight_hbm.1, bf16[2048,128]{1,0:T(8,128)(2,1)S(1)} %copy.9.down, f32[512,128]{1,0:T(8,128)S(1)} %compare_convert_fusion.mask, ...), custom_call_target="tpu_custom_call" | custom-call | flops 4294967296 | bytes 8388608 | tf_op jit(solution)/shard_map/pallas_call | solution.py:350
  72.8 0.8 %copy.13 = bf16[128,2048]{1,0:T(8,128)(2,1)} copy(bf16[128,2048]{1,0:T(8,128)(2,1)S(1)} %shard_map.73) | data formatting | bytes 1048576
  (4 shorter events, 0.0 us)
Async XLA Ops:
  0.0 2.2 %copy-start = (bf16[8,16,2048]{2,1,0:T(8,128)(2,1)S(1)}, bf16[8,16,2048]{2,1,0:T(8,128)(2,1)}, u32[]{:S(2)}) copy-start(bf16[8,16,2048]{2,1,0:T(8,128)(2,1)} %param.13) | copy-start | bytes 1572868
  5.5 0.7 copy-start.1

commit v6 on v5

--- a/solution.py
+++ b/solution.py
@@ -66,8 +66,8 @@
 
 def project_kernel(
     nt, np_, chunks,
-    lengths, queries, cache, weight_hbm, down, mask, up_mine, out,
-    kv_buf, kv_sem, weight, weight_sem, full, total, inbox, outbox, ups, shr, shr_in, shr_sum, shr_peer,
+    lengths, queries, cache, weight_hbm, down, slots, up_all, out,
+    up_mine, kv_buf, kv_sem, weight, weight_sem, full, total, inbox, outbox, ups, shr, shr_in, shr_sum, shr_peer,
     att_send, att_recv, core_send, core_recv, hop_send, hop_recv,
     up_send, up_recv, one_send, one_recv, two_send, two_recv,
 ):
@@ -107,6 +107,8 @@
     pl.semaphore_wait(barrier, nt + np_ - 2)
 
     other = t + 1 - 2 * (t % 2)
+    for b in range(rows // BLK):
+        up_mine[b] = up_all[slots[b]]
     sends = []
     for k in range(1, np_):
         q = (p + k) % np_
@@ -168,7 +170,16 @@
     def shrink(j):
         at = slice(j * half, (j + 1) * half)
         part = jnp.dot(full[at, :], down[...], preferred_element_type=jnp.float32)
-        part = jnp.where(mask[at, :] > 0, part, 0.0).astype(jnp.bfloat16)
+        rank = np_ * up_mine.shape[1]
+        lane_slot = lax.broadcasted_iota(jnp.int32, (piece, part.shape[1]), 1) // rank
+        lane_slot = lane_slot + t * (part.shape[1] // rank)
+        part = jnp.concatenate(
+            [
+                jnp.where(lane_slot == slots[b], part[b * piece : (b + 1) * piece], 0.0)
+                for b in range(rows // BLK)
+            ],
+            axis=0,
+        ).astype(jnp.bfloat16)
         for q in range(np_):
             shr[q, j * part_share : (j + 1) * part_share, :] = part[q * part_share : (q + 1) * part_share]
 
@@ -337,12 +348,7 @@
         chunks = max(1, min(4, columns // 512))
         wide = columns // chunks
         lanes = slots * rank
-        t = lax.axis_index("tensor")
         down = jnp.transpose(adapter_down_weight, (1, 0, 2)).reshape(feat, lanes)
-        row_slots = jnp.tile(jnp.repeat(block_adapter_slot, BLK // PIECES), PIECES)
-        lane_slots = t * slots + jnp.arange(lanes, dtype=jnp.int32) // rank
-        mask = (row_slots[:, None] == lane_slots[None, :]).astype(jnp.float32)
-        up_mine = jnp.take(adapter_up_weight, block_adapter_slot, axis=0)
         per_share = share // BLK
         bf = jnp.bfloat16
         dma = pltpu.SemaphoreType.DMA
@@ -356,9 +362,14 @@
                 pl.BlockSpec(memory_space=pl.ANY),
                 pl.BlockSpec(memory_space=pl.ANY),
             ]
-            + [pl.BlockSpec(memory_space=pltpu.VMEM)] * 3,
+            + [
+                pl.BlockSpec(memory_space=pltpu.VMEM),
+                pl.BlockSpec(memory_space=pltpu.SMEM),
+                pl.BlockSpec(memory_space=pltpu.VMEM),
+            ],
             out_specs=pl.BlockSpec(memory_space=pltpu.VMEM),
             scratch_shapes=[
+                pltpu.VMEM((rows // BLK,) + adapter_up_weight.shape[1:], bf),
                 pltpu.VMEM((2, STEP) + key_value_cache.shape[1:], bf),
                 dma((2,)),
                 pltpu.VMEM((feat, columns), bf),
@@ -367,7 +378,7 @@
                 pltpu.VMEM((rows, columns), jnp.float32),
                 pltpu.VMEM(boxes, bf),
                 pltpu.VMEM(boxes, bf),
-                pltpu.VMEM((np_, per_share, up_mine.shape[1], columns), bf),
+                pltpu.VMEM((np_, per_share, adapter_up_weight.shape[1], columns), bf),
                 pltpu.VMEM((np_, share, lanes), bf),
                 pltpu.VMEM((np_, share, lanes), bf),
                 pltpu.VMEM((share, lanes), bf),
@@ -385,7 +396,7 @@
             ),
         )(
             cache_lengths, queries.reshape(block, feat // HD, HD), key_value_cache, output_weight,
-            down, mask, up_mine,
+            down, block_adapter_slot, adapter_up_weight,
         )
 
     return local

time: 73.9 us -> 72.8 us (0.985)
  other arithmetic: 1.61 us -> 0 us
    unnamed x8, local copies, waits for them, and re-layouts: 2.61 us -> 4.29 us
    select_n x2 -> x0, other arithmetic: 0.75 us -> none  [local(): up_mine = jnp.take(adapter_up_weight, block_adapter_slot, axis=0)]
where the time goes in v6:
time: 72.8 us; the launch traced here: 72.4 us
  Pallas kernels  66.8 us (92%)
  local copies, waits for them, and re-layouts  5.6 us (8%)
    pallas_call x1, Pallas kernels, local(): pl.pallas_call(functools.partial(project_kernel, nt, np_, chunks), out_sh...  66.8 us
    unnamed x8, local copies, waits for them, and re-layouts  4.29 us

profile of v6, /device:TPU:0, one launch (start us, length us, event | category | flops | bytes accessed | tf_op | source)
XLA Modules:
  0.0 72.4 jit_solution(1235356761709759483)
XLA Ops:
  0.0 1.1 %copy.10 = bf16[16,8,16,128]{3,2,1,0:T(8,128)(2,1)S(1)} copy(bf16[16,8,16,128]{3,1,2,0:T(8,128)(2,1)} %bitcast.6) | data formatting | bytes 1048576
  1.2 1.3 %copy.9.down = bf16[2048,128]{1,0:T(8,128)(2,1)S(1)} copy(bf16[2048,128]{0,1:T(8,128)(2,1)} %bitcast.7) | data formatting | bytes 1048576 | tf_op jit(solution)/shard_map/reshape | solution.py:351
  2.5 0.0 copy-start
  2.5 1.0 %copy-done = bf16[8,16,2048]{2,1,0:T(8,128)(2,1)S(1)} copy-done((bf16[8,16,2048]{2,1,0:T(8,128)(2,1)S(1)}, bf16[8,16,2048]{2,1,0:T(8,128)(2,1)}, u32[]{:S(2)}) %copy-start) | copy-done | bytes 524312
  3.5 0.0 copy-start.1
  3.5 0.7 copy-done.1
  4.2 0.0 copy-start.2
  4.2 0.7 copy-done.2
  4.8 66.8 %shard_map.73 = bf16[128,2048]{1,0:T(8,128)(2,1)S(1)} custom-call(s32[128]{0:T(128)S(1)} %copy-done.1, bf16[128,16,128]{2,1,0:T(8,128)(2,1)S(1)} %bitcast.5, bf16[128,128,2,256]{3,2,1,0:T(2,128)(2,1)} %cache.1, bf16[2048,2048]{1,0:T(8,128)(2,1)} %weight_hbm.1, bf16[2048,128]{1,0:T(8,128)(2,1)S(1)} %copy.9.down, s32[4]{0:T(128)S(1)} %copy-done.2, ...), custom_call_target="tpu_custom_call" | custom-call | flops 4294967296 | bytes 8388608 | tf_op jit(solution)/shard_map/pallas_call | solution.py:356
  71.6 0.8 %copy.12 = bf16[128,2048]{1,0:T(8,128)(2,1)} copy(bf16[128,2048]{1,0:T(8,128)(2,1)S(1)} %shard_map.73) | data formatting | bytes 1048576
Async XLA Ops:
  2.5 1.0 %copy-start = (bf16[8,16,2048]{2,1,0:T(8,128)(2,1)S(1)}, bf16[8,16,2048]{2,1,0:T(8,128)(2,1)}, u32[]{:S(2)}) copy-start(bf16[8,16,2048]{2,1,0:T(8,128)(2,1)} %up_all.1) | copy-start | bytes 1572868
  3.5 0.7 copy-start.1
  4.2 0.7 copy-start.2
